TPU v7x, 32 devices: a whole 2x2x4 slice. The times are simulated.
32 devices in a mesh: batch: 4 (over z), proto: 8 (over y, x, core).
Axes of the slice: x: 2, y: 2, z: 4, core: 2. Of those that a mesh axis runs over, the one named last changes fastest.
Arguments:
- teacher: bfloat16 [16, 256, 256], P('batch'), may hold values from -1 to 1
- student: bfloat16 [16, 256, 256], P('batch'), may hold values from -0.5 to 0.5
- perm: int32 [16, 256], P('batch'), may hold values from 0 to 255, each once within a row
- counts: int32 [4, 4], P('batch'), may hold values from 1 to 128, 384 in all within a row
- prototypes: bfloat16 [256, 131072], P(None, 'proto'), may hold values from -1 to 1
Outputs:
- feature_grad: float32 [1536, 256], P(('batch', 'proto'))
- proto_grad: float32 [256, 131072], P('batch', 'proto')
Inputs may be any that keep to these rules, and one draw needn't show every extreme that they name: Each row of counts sums to exactly 384; some image of each batch index has exactly 128 masked patches. Each row of perm is a permutation of the 256 patches; the first counts entries of an image's row are its masked patches.
All inputs are finite; a program needn't handle non-finite values.
Results may differ from a plain program's by a relative error of at most 0.0053.
Values sent between devices are 32-bit elements; how exact they have to be, the bound alone decides.
A program may use at most 128 MiB of HBM per device.

v0:
```python
import jax
import jax.numpy as jnp
from jax import lax
from jax.sharding import PartitionSpec as P

K = 131072
SWEEPS = 3
GROUP_ROWS = 384


def unit_rows(rows):
    values = rows.astype(jnp.float32)
    inverse = lax.rsqrt(jnp.sum(values * values, axis=1, keepdims=True) + 1e-06)
    return (values * inverse, inverse)


def row_total(partial_value):
    return lax.psum(partial_value, "proto")


def on_device(teacher, student, perm, counts, prototypes):
    img_count = teacher.shape[0]
    patches = teacher.shape[1]
    width = teacher.shape[2]
    group_rows = GROUP_ROWS
    tally = counts.reshape(-1)
    ends = jnp.cumsum(tally)
    starts = ends - tally
    line = jnp.arange(group_rows, dtype=jnp.int32)
    owner = jnp.sum((ends[None, :] <= line[:, None]).astype(jnp.int32), axis=1)
    picked = owner[:, None] == jnp.arange(img_count, dtype=jnp.int32)[None, :]
    first = jnp.sum(jnp.where(picked, starts[None, :], 0), axis=1)
    owned = jnp.sum(jnp.where(picked, tally[None, :], 0), axis=1)
    inner = line - first
    packed_patch = jnp.take(perm.reshape(-1), owner * patches + inner)
    packed_flat = owner * patches + packed_patch
    live = jnp.ones((group_rows,), jnp.float32)
    weight_row = 1.0 / owned.astype(jnp.float32)
    teach_flat = teacher.reshape(-1, width)
    stud_flat = student.reshape(-1, width)
    teach_unit, unused = unit_rows(jnp.take(teach_flat, packed_flat, axis=0))
    stud_unit, unused_inv = unit_rows(jnp.take(stud_flat, packed_flat, axis=0))
    teach_half = teach_unit.astype(jnp.bfloat16)
    stud_half = stud_unit.astype(jnp.bfloat16)
    energy = jnp.exp(jnp.dot(teach_half, prototypes, preferred_element_type=jnp.float32) * 25.0)
    expo = jnp.exp(jnp.dot(stud_half, prototypes, preferred_element_type=jnp.float32) * 10.0)
    soft_part = jnp.sum(expo, axis=1)
    row_scale = live
    col_scale = jnp.ones((energy.shape[1],), jnp.float32)
    for sweep in range(SWEEPS):
        col_part = jnp.dot(row_scale, energy, precision=lax.Precision.HIGHEST)
        col_scale = 1.0 / lax.psum(col_part, "batch")
        row_part = jnp.dot(energy, col_scale, precision=lax.Precision.HIGHEST)
        rows_sum = row_total(row_part)
        row_scale = live / rows_sum
    soft_total = lax.psum(soft_part, "proto")
    soft = expo / soft_total[:, None]
    target = row_scale[:, None] * energy * col_scale[None, :]
    grad = (K * 10.0 * weight_row[:, None] * (soft - target)).astype(jnp.bfloat16)
    proto_grad = lax.psum_scatter(
        lax.dot_general(
            stud_half, grad, (((0,), (0,)), ((), ())), preferred_element_type=jnp.float32
        ),
        "batch",
        scatter_dimension=0,
        tiled=True,
    )
    share = group_rows // lax.axis_size("proto")
    back = lax.psum_scatter(
        lax.dot_general(
            grad, prototypes, (((1,), (1,)), ((), ())), preferred_element_type=jnp.float32
        ),
        "proto",
        scatter_dimension=0,
        tiled=True,
    )
    begin = lax.axis_index("proto") * share
    mine = lax.dynamic_slice_in_dim(packed_flat, begin, share, 0)
    own_unit, own_inverse = unit_rows(jnp.take(stud_flat, mine, axis=0))
    feature_grad = own_inverse * (back - own_unit * jnp.sum(own_unit * back, axis=1, keepdims=True))
    return (feature_grad, proto_grad)


def solution(mesh):
    in_specs = (
        P("batch", None, None),
        P("batch", None, None),
        P("batch", None),
        P("batch", None),
        P(None, "proto"),
    )
    out_specs = (P(("batch", "proto"), None), P("batch", "proto"))
    return jax.shard_map(
        on_device, mesh=mesh, in_specs=in_specs, out_specs=out_specs, check_vma=False
    )
```

profile of v0, /device:TPU:7, one launch (start us, length us, event | category | flops | bytes accessed | tf_op | source)
XLA Modules:
  0.0 641.0 jit_solution(4663297708271389111)
XLA Ops:
  7.2 0.0 copy-start
  7.2 0.0 all-reduce.5.cloned.1.call-start
  7.2 0.9 reduce-window.4
  8.1 0.7 fusion.15
  8.8 0.1 convert_reduce_fusion
  8.9 0.7 select_reduce_fusion
  9.6 0.7 copy.7
  10.3 1.9 gather_fusion
  12.3 0.0 copy-done
  12.3 2.1 gather_fusion.2
  14.3 2.8 gather_fusion.3
  17.1 0.3 fusion
  17.4 14.2 %multiply_exponential_fusion = f32[384,16384]{1,0:T(8,128)} fusion(bf16[256,16384]{1,0:T(8,128)(2,1)} %param.11, f32[384]{0:T(512)S(1)} %add_rsqrt_fusion, bf16[384,256]{1,0:T(8,128)(2,1)S(1)} %gather_fusion.3, pred[384]{0:T(512)(128)(4,1)S(1)} %get-tuple-element.11), kind=kOutput, calls=%fused_computation.5 | convolution fusion | flops 3227910144 | bytes 33752960 | tf_op jit(solution)/shard_map/dot_general | solution.py:45
  31.7 16.2 %fusion.13 = f32[1,16384]{1,0:T(1,128)} fusion(f32[384,16384]{1,0:T(8,128)} %multiply_exponential_fusion), kind=kOutput, calls=%fused_computation.56 | convolution fusion | flops 75497472 | bytes 25231360 | tf_op jit(solution)/shard_map/dot_general | solution.py:51
  47.9 0.0 all-reduce.5.cloned.1.call-update
  47.9 0.2 all-reduce.7.cloned.1.call-start
  48.1 33.1 %all-reduce.5.cloned.1.call-done = f32[16384]{0:T(1024)} async-done(((f32[16384]{0:T(1024)}), f32[16384]{0:T(1024)}) %all-reduce.5.cloned.1.call-update) | async-done | bytes 65552 | tf_op jit(solution)/shard_map/psum | solution.py:52
  81.3 0.9 broadcast_divide_fusion.2
  82.1 23.7 %convolution_reduce_fusion.2 = f32[384]{0:T(512)S(1)} fusion(f32[384,16384]{1,0:T(8,128)} %multiply_exponential_fusion, f32[16384,1]{0,1:T(1,128)S(1)} %bitcast.43), kind=kOutput, calls=%fused_computation.9 | convolution fusion | flops 75497472 | bytes 25232896 | tf_op jit(solution)/shard_map/dot_general | solution.py:53
  105.9 12.0 %psum.51 = f32[384]{0:T(512)S(1)} all-reduce(f32[384]{0:T(512)S(1)} %convolution_reduce_fusion.2), channel_id=1, replica_groups=mesh['batch'=4,'proto'=8] {'proto'}, use_global_device_ids=true, to_apply=%region_10.12 | all-reduce | flops 384 | bytes 3072 | tf_op jit(solution)/shard_map/psum | solution.py:18
  117.9 16.2 %fusion.22 = f32[1,16384]{1,0:T(1,128)} fusion(f32[384,1]{0,1:T(1,128)S(1)} %reshape.150, f32[384,16384]{1,0:T(8,128)} %multiply_exponential_fusion), kind=kOutput, calls=%fused_computation.65 | convolution fusion | flops 75497472 | bytes 25232896 | tf_op jit(solution)/shard_map/dot_general | solution.py:51
  134.1 0.0 all-reduce.7.cloned.1.call-update
  134.1 0.3 all-reduce.9.cloned.1.call-start
  134.4 14.5 %fusion.21 = (f32[384]{0:T(512)S(1)}, f32[384,16384]{1,0:T(8,128)}) fusion(bf16[256,16384]{1,0:T(8,128)(2,1)} %param.11, f32[384]{0:T(512)S(1)} %add_rsqrt_fusion.1, bf16[384,256]{1,0:T(8,128)(2,1)S(1)} %gather_fusion.2, pred[384]{0:T(512)(128)(4,1)S(1)} %get-tuple-element.11), kind=kOutput, calls=%fused_computation.64 | convolution fusion | flops 3234201088 | bytes 33754496 | tf_op jit(solution)/shard_map/dot_general | solution.py:46
  148.9 17.9 %all-reduce.7.cloned.1.call-done = f32[16384]{0:T(1024)} async-done(((f32[16384]{0:T(1024)}), f32[16384]{0:T(1024)}) %all-reduce.7.cloned.1.call-update) | async-done | bytes 65552 | tf_op jit(solution)/shard_map/psum | solution.py:52
  166.9 0.9 broadcast_divide_fusion.1
  167.7 23.7 %convolution_reduce_fusion.1 = f32[384]{0:T(512)S(1)} fusion(f32[384,16384]{1,0:T(8,128)} %multiply_exponential_fusion, f32[16384,1]{0,1:T(1,128)S(1)} %bitcast.44), kind=kOutput, calls=%fused_computation.8 | convolution fusion | flops 75497472 | bytes 25232896 | tf_op jit(solution)/shard_map/dot_general | solution.py:53
  191.5 12.0 %psum.53 = f32[384]{0:T(512)S(1)} all-reduce(f32[384]{0:T(512)S(1)} %convolution_reduce_fusion.1), channel_id=1, replica_groups=mesh['batch'=4,'proto'=8] {'proto'}, use_global_device_ids=true, to_apply=%region_12.14 | all-reduce | flops 384 | bytes 3072 | tf_op jit(solution)/shard_map/psum | solution.py:18
  203.5 16.2 %fusion.23 = f32[1,16384]{1,0:T(1,128)} fusion(f32[384,1]{0,1:T(1,128)S(1)} %reshape.154, f32[384,16384]{1,0:T(8,128)} %multiply_exponential_fusion), kind=kOutput, calls=%fused_computation.66 | convolution fusion | flops 75497472 | bytes 25232896 | tf_op jit(solution)/shard_map/dot_general | solution.py:51
  219.7 0.0 all-reduce.9.cloned.1.call-update
  219.8 0.3 reduce-scatter.3.cloned.1.call-start
  220.1 32.4 %all-reduce.9.cloned.1.call-done = f32[16384]{0:T(1024)} async-done(((f32[16384]{0:T(1024)}), f32[16384]{0:T(1024)}) %all-reduce.9.cloned.1.call-update) | async-done | bytes 65552 | tf_op jit(solution)/shard_map/psum | solution.py:52
  252.5 0.9 broadcast_divide_fusion
  253.4 23.7 %convolution_reduce_fusion = f32[384]{0:T(512)S(1)} fusion(f32[384,16384]{1,0:T(8,128)} %multiply_exponential_fusion, f32[16384,1]{0,1:T(1,128)S(1)} %bitcast.39), kind=kOutput, calls=%fused_computation.7 | convolution fusion | flops 75497472 | bytes 25232896 | tf_op jit(solution)/shard_map/dot_general | solution.py:53
  277.1 12.0 %all-reduce = (f32[384]{0:T(512)S(1)}, f32[384]{0:T(512)S(1)}) all-reduce(f32[384]{0:T(512)S(1)} %convolution_reduce_fusion, f32[384]{0:T(512)S(1)} %get-tuple-element.13), channel_id=1, replica_groups=mesh['batch'=4,'proto'=8] {'proto'}, use_global_device_ids=true, to_apply=%region_14.16 | all-reduce | flops 768 | bytes 6144 | tf_op jit(solution)/shard_map/psum | solution.py:18
  289.1 16.5 %multiply_convert_fusion = bf16[384,16384]{1,0:T(8,128)(2,1)S(1)} fusion(f32[384,16384]{1,0:T(8,128)} %multiply_exponential_fusion, f32[384,16384]{1,0:T(8,128)} %get-tuple-element.14, f32[16384]{0:T(1024)S(1)} %broadcast_divide_fusion, f32[384]{0:T(512)S(1)} %broadcast_divide_fusion.5, f32[384]{0:T(512)S(1)} %get-tuple-element.8, f32[384]{0:T(512)S(1)} %divide_multiply_fusion), kind=kLoop, calls=%fused_computation.4 | loop fusion | flops 37748736 | bytes 62984704 | tf_op jit(solution)/shard_map/convert_element_type | solution.py:59
  305.6 0.0 copy-start.1
  305.7 4.6 copy-done.1
  310.2 6.6 %fusion.24 = f32[384,256]{1,0:T(8,128)} fusion(bf16[384,16384]{1,0:T(8,128)(2,1)S(1)} %multiply_convert_fusion, bf16[256,16384]{1,0:T(8,128)(2,1)} %param.11), kind=kOutput, calls=%fused_computation.67 | convolution fusion | flops 3221225472 | bytes 21364736 | tf_op jit(solution)/shard_map/dot_general | solution.py:70
  316.8 0.0 reduce-scatter.3.cloned.1.call-update
  316.9 0.0 reduce-scatter.5.cloned.1.call-start
  316.9 12.9 %fusion.18 = f32[256,16384]{1,0:T(8,128)} fusion(bf16[384,16384]{1,0:T(8,128)(2,1)} %copy-done.1, f32[384]{0:T(512)S(1)} %add_rsqrt_fusion.1, bf16[384,256]{1,0:T(8,128)(2,1)S(1)} %gather_fusion.2, pred[384]{0:T(512)(128)(4,1)S(1)} %get-tuple-element.11), kind=kOutput, calls=%fused_computation.63 | convolution fusion | flops 3221618688 | bytes 29558656 | tf_op jit(solution)/shard_map/dot_general | solution.py:61
  329.8 0.0 reduce-scatter.5.cloned.1.call-update
  329.9 0.1 compare_and_fusion.1
  330.0 0.7 gather_fusion.1
  330.6 0.2 fusion.11
  330.8 19.2 %reduce-scatter.3.cloned.1.call-done = f32[48,256]{1,0:T(8,128)} async-done(((f32[384,256]{1,0:T(8,128)}), f32[48,256]{1,0:T(8,128)}) %reduce-scatter.3.cloned.1.call-update) | async-done | bytes 49168 | tf_op jit(solution)/shard_map/reduce_scatter | solution.py:69
  350.0 1.0 fusion.8
  351.0 1.5 fusion.10
  352.5 282.0 %reduce-scatter.5.cloned.1.call-done = f32[64,16384]{1,0:T(8,128)} async-done(((f32[256,16384]{1,0:T(8,128)}), f32[64,16384]{1,0:T(8,128)}) %reduce-scatter.5.cloned.1.call-update) | async-done | bytes 4194320 | tf_op jit(solution)/shard_map/reduce_scatter | solution.py:60
  (16 shorter events, 0.1 us)
Async XLA Ops:
  7.2 5.1 copy-start
  7.2 74.1 %all-reduce.5.cloned.1.call-start = ((), (), s32[]{:S(2)}) async-start(), calls=%async_computation.2 | async-start | bytes 131072 | tf_op jit(solution)/shard_map/psum | solution.py:52
  47.9 119.0 %all-reduce.7.cloned.1.call-start = ((), (), s32[]{:S(2)}) async-start(), calls=%async_computation.3 | async-start | bytes 131072 | tf_op jit(solution)/shard_map/psum | solution.py:52
  134.1 118.4 %all-reduce.9.cloned.1.call-start = ((), (), s32[]{:S(2)}) async-start(), calls=%async_computation.4 | async-start | bytes 131072 | tf_op jit(solution)/shard_map/psum | solution.py:52
  219.8 130.2 %reduce-scatter.3.cloned.1.call-start = ((), (), s32[]{:S(2)}) async-start(), calls=%async_computation.5 | async-start | bytes 442368 | tf_op jit(solution)/shard_map/reduce_scatter | solution.py:69
  305.6 4.6 copy-start.1
  316.9 317.6 %reduce-scatter.5.cloned.1.call-start = ((), (), s32[]{:S(2)}) async-start(), calls=%async_computation.6 | async-start | bytes 20971520 | tf_op jit(solution)/shard_map/reduce_scatter | solution.py:60
Sparse Core Ops, SparseCore 0:
  48.0 33.1 all-reduce.4
  134.3 32.5 all-reduce.6
  219.9 32.5 all-reduce.8
  317.0 32.9 reduce-scatter.2
  352.9 281.5 reduce-scatter.4
where the time goes:
time: 643 us; the launch traced here: 641 us
  waiting for transfers between devices  385 us (60%)
  matrix products  168 us (26%)
  blocking collectives  36.1 us (6%)
  other arithmetic  24.6 us (4%)
  between operations  13.9 us (2%)
  local copies, waits for them, and re-layouts  12.7 us (2%)
    reduce_scatter x1, waiting for transfers between devices, on_device(): lax.psum_scatter(lax.dot_general(stud_half, grad, (((0,), (0,)), ((), ())...  282 us
    psum x3, waiting for transfers between devices, on_device(): col_scale = 1.0 / lax.psum(col_part, 'batch')  83.5 us
    dot_general x3, matrix products, on_device(): row_part = jnp.dot(energy, col_scale, precision=lax.Precision.HIGHEST)  71.2 us
    dot_general x3, matrix products, on_device(): col_part = jnp.dot(row_scale, energy, precision=lax.Precision.HIGHEST)  48.7 us
    psum x3, blocking collectives, row_total(): return lax.psum(partial_value, 'proto')  36.1 us
    reduce_scatter x1, waiting for transfers between devices, on_device(): lax.psum_scatter(lax.dot_general(grad, prototypes, (((1,), (1,)), ((), ()...  19.2 us
    convert_element_type x1, other arithmetic, on_device(): (K * 10.0 * weight_row[:, None] * (soft - target)).astype(jnp.bfloat16)  16.5 us
    dot_general x1, matrix products, on_device(): jnp.dot(stud_half, prototypes, preferred_element_type=jnp.float32) * 10.0  14.5 us
  transfers between devices with their start and end apart: 5, of which 5 were waited for; matrix products, arithmetic and copies ran while one was open for 5% of the time, Pallas kernels for 0%

commit v1 on v0

v1 whole, which is shorter than its diff:
```python
import functools
import math
import jax
import jax.numpy as jnp
from jax import lax
from jax.experimental import pallas as pl
from jax.experimental.pallas import tpu as pltpu
from jax.sharding import PartitionSpec as P

K = 131072
SWEEPS = 3
GROUP_ROWS = 384
LOG2E = 1.4426950408889634
MESH = pl.DeviceIdType.MESH
NT = (((1,), (1,)), ((), ()))


def unit_rows(rows):
    values = rows.astype(jnp.float32)
    inverse = lax.rsqrt(jnp.sum(values * values, axis=1, keepdims=True) + 1e-06)
    return (values * inverse, inverse)


def ring(n, stage, me, buf, send, recv, device):
    copies = []
    for d in range(1, n):
        copies.append(pltpu.make_async_remote_copy(
            src_ref=buf.at[me], dst_ref=buf.at[me], send_sem=send.at[stage, d], recv_sem=recv.at[stage, d],
            device_id=device(lax.rem(me + d, n)), device_id_type=MESH))
    for copy in copies:
        copy.start()
    for copy in copies:
        copy.wait()
    total = buf[0]
    for d in range(1, n):
        total = total + buf[d]
    return total


def scores(weights_t, rows_ref):
    return lax.dot_general(weights_t, rows_ref[...], NT, preferred_element_type=jnp.float32)


def sinkhorn_kernel(nb, np_, cols, step, teach, stud, proto, out, energy, wbuf, tbuf, sbuf, acc, acc2, wsem,
                    p0, p1, p2, q0, q1, q2, psend, precv, qsend, qrecv):
    b, p = lax.axis_index("batch"), lax.axis_index("proto")
    rows = teach.shape[0]
    load = pltpu.make_async_copy(proto.at[:, pl.ds(pl.multiple_of(b * cols, cols), cols)], wbuf, wsem)
    load.start()
    barrier = pltpu.get_barrier_semaphore()
    for d in range(1, np_):
        pl.semaphore_signal(barrier, inc=1, device_id=(b, lax.rem(p + d, np_)), device_id_type=MESH)
    for d in range(1, nb):
        pl.semaphore_signal(barrier, inc=1, device_id=(lax.rem(b + d, nb), p), device_id_type=MESH)
    pl.semaphore_wait(barrier, np_ + nb - 2)
    load.wait()
    acc[...] = jnp.zeros_like(acc)
    acc2[...] = jnp.zeros_like(acc2)

    def first(i, carry):
        wt = wbuf[:, pl.ds(pl.multiple_of(i * step, step), step)].T
        tbuf[...] = scores(wt, teach)
        sbuf[...] = scores(wt, stud)
        row = acc[...]
        row2 = acc2[...]
        for g in range(0, step, 8):
            e = jnp.exp2(tbuf[g:g + 8, :] * (25.0 * LOG2E))
            energy[pl.ds(pl.multiple_of(i * step + g, 8), 8), :] = e
            row = row + e * (1.0 / jnp.sum(e, axis=1, keepdims=True))
            row2 = row2 + jnp.exp2(sbuf[g:g + 8, :] * (10.0 * LOG2E))
        acc[...] = row
        acc2[...] = row2
        return carry

    lax.fori_loop(0, cols // step, first, 0)

    def reduce(stage, value, pbuf, qbuf):
        pbuf[p] = value
        part = ring(np_, stage, p, pbuf, psend, precv, lambda other: (b, other))
        qbuf[b] = part
        return ring(nb, stage, b, qbuf, qsend, qrecv, lambda other: (other, p))

    value = jnp.concatenate([jnp.sum(acc[...], axis=0, keepdims=True), jnp.sum(acc2[...], axis=0, keepdims=True)], axis=1)
    total = reduce(0, value, p0, q0)
    out[0:1, :] = total[:, rows:]
    scale = 1.0 / total[:, :rows]
    for sweep in range(1, SWEEPS):
        out[2 * sweep - 1:2 * sweep, :] = scale
        wide = jnp.broadcast_to(scale, (8, rows))

        def body(i, row):
            for g in range(0, 128, 8):
                e = energy[pl.ds(pl.multiple_of(i * 128 + g, 8), 8), :]
                row = row + e * (1.0 / jnp.sum(e * wide, axis=1, keepdims=True))
            return row

        row = lax.fori_loop(0, cols // 128, body, jnp.zeros((8, rows), jnp.float32))
        total = reduce(sweep, jnp.sum(row, axis=0, keepdims=True), (p0, p1, p2)[sweep], (q0, q1, q2)[sweep])
        scale = 1.0 / total
    out[2 * SWEEPS - 1:2 * SWEEPS, :] = scale


def gradient_kernel(nb, np_, half, step, share, teach, stud, stud_t, vec, proto, out, back_out,
                    wbuf, tbuf, sbuf, gbuf, own, away, back, parts, mine_buf, wsem, osem, asend, arecv, bsend, brecv):
    b, p = lax.axis_index("batch"), lax.axis_index("proto")
    rows = teach.shape[0]
    h = lax.rem(b, 2)
    pair = b - h
    other = pair + 1 - h
    pair_rows = 2 * np_ * share
    block = out.shape[0]
    base = h * half
    load = pltpu.make_async_copy(proto.at[:, pl.ds(pl.multiple_of(base, half), half)], wbuf, wsem)
    load.start()
    barrier = pltpu.get_barrier_semaphore()
    for d in range(1, np_):
        peer = lax.rem(p + d, np_)
        pl.semaphore_signal(barrier, inc=1, device_id=(b, peer), device_id_type=MESH)
        pl.semaphore_signal(barrier, inc=1, device_id=(other, peer), device_id_type=MESH)
    pl.semaphore_signal(barrier, inc=1, device_id=(other, p), device_id_type=MESH)
    pl.semaphore_wait(barrier, 2 * np_ - 1)
    load.wait()
    back[...] = jnp.zeros_like(back)
    scale_prev, target_scale, soft_scale = vec[0:1, :], vec[1:2, :], vec[2:3, :]

    def body(i, carry):
        cols = pl.ds(pl.multiple_of(i * step, step), step)
        w = wbuf[:, cols]
        wt = w.T
        tbuf[...] = scores(wt, teach)
        sbuf[...] = scores(wt, stud)
        for g in range(0, step, 16):
            e = jnp.exp2(tbuf[g:g + 16, :] * (25.0 * LOG2E))
            c = 1.0 / jnp.sum(e * scale_prev, axis=1, keepdims=True)
            soft = jnp.exp2(sbuf[g:g + 16, :] * (10.0 * LOG2E)) * soft_scale
            gbuf[g:g + 16, :] = (soft - e * target_scale * c).astype(jnp.bfloat16)
        res = lax.dot_general(stud_t[...], gbuf[...], NT, preferred_element_type=jnp.float32)
        own[:, cols] = res[:block]
        away[:, cols] = res[block:]
        there = pl.ds(pl.multiple_of(base + i * step, step), step)
        pltpu.make_async_remote_copy(
            src_ref=away.at[:, cols], dst_ref=out.at[:, there], send_sem=asend, recv_sem=arecv,
            device_id=(other, p), device_id_type=MESH).start()
        pltpu.make_async_copy(own.at[:, cols], out.at[:, there], osem).start()
        part = gbuf[:, pl.ds(pl.multiple_of((b // 2) * pair_rows, pair_rows), pair_rows)]
        back[...] += jnp.dot(w, part, preferred_element_type=jnp.float32)
        return carry

    lax.fori_loop(0, half // step, body, 0)
    full = back[...].T
    for s in range(2 * np_):
        parts[s, 0:share, :] = full[s * share:(s + 1) * share, :]
    copies = []
    slot = h * np_ + p
    for d in range(1, 2 * np_):
        to = lax.rem(slot + d, 2 * np_)
        copies.append(pltpu.make_async_remote_copy(
            src_ref=parts.at[to], dst_ref=mine_buf.at[d],
            send_sem=bsend.at[d], recv_sem=brecv.at[d],
            device_id=(pair + to // np_, lax.rem(to, np_)), device_id_type=MESH))
    for copy in copies:
        copy.start()
    total = parts[slot]
    for copy in copies:
        copy.wait()
    for d in range(1, 2 * np_):
        total = total + mine_buf[d]
    back_out[...] = total[:share]
    there = pl.ds(pl.multiple_of(base, half), half)
    pltpu.make_async_copy(own, out.at[:, there], osem).wait()
    arrive = pl.ds(pl.multiple_of(half - base, half), half)
    whole = pltpu.make_async_remote_copy(
        src_ref=away, dst_ref=out.at[:, arrive], send_sem=asend, recv_sem=arecv,
        device_id=(other, p), device_id_type=MESH)
    whole.wait()


def on_device(nb, np_, teacher, student, perm, counts, prototypes):
    img_count = teacher.shape[0]
    patches = teacher.shape[1]
    width = teacher.shape[2]
    group_rows = GROUP_ROWS
    rows = nb * group_rows
    share = group_rows // np_
    local = prototypes.shape[1]
    b, p = lax.axis_index("batch"), lax.axis_index("proto")
    tally = counts.reshape(-1)
    ends = jnp.cumsum(tally)
    starts = ends - tally
    line = p * share + jnp.arange(share, dtype=jnp.int32)
    owner = jnp.sum((ends[None, :] <= line[:, None]).astype(jnp.int32), axis=1)
    picked = owner[:, None] == jnp.arange(img_count, dtype=jnp.int32)[None, :]
    first = jnp.sum(jnp.where(picked, starts[None, :], 0), axis=1)
    owned = jnp.sum(jnp.where(picked, tally[None, :], 0), axis=1)
    inner = line - first
    flat = owner * patches + jnp.take(perm.reshape(-1), owner * patches + inner)
    teach_unit, unused = unit_rows(jnp.take(teacher.reshape(-1, width), flat, axis=0))
    own_unit, own_inverse = unit_rows(jnp.take(student.reshape(-1, width), flat, axis=0))
    weight = jnp.broadcast_to((K * 10.0) * (1.0 / owned.astype(jnp.float32))[:, None], (share, 128))
    packed = jnp.concatenate(
        [teach_unit.astype(jnp.bfloat16).astype(jnp.float32), own_unit.astype(jnp.bfloat16).astype(jnp.float32), weight], axis=1)
    gathered = lax.all_gather(packed, ("batch", "proto"), axis=0, tiled=True)
    teach = gathered[:, :width].astype(jnp.bfloat16)
    stud = gathered[:, width:2 * width].astype(jnp.bfloat16)
    weight_row = gathered[:, 2 * width].reshape(1, rows)

    cols = local // nb
    step = min(256, cols)
    vmem = pltpu.VMEM
    f32 = jnp.float32
    dma = pltpu.SemaphoreType.DMA
    whole = pl.BlockSpec(memory_space=vmem)
    sums = pl.pallas_call(
        functools.partial(sinkhorn_kernel, nb, np_, cols, step),
        out_shape=jax.ShapeDtypeStruct((8, rows), f32),
        in_specs=[whole, whole, pl.BlockSpec(memory_space=pl.ANY)],
        out_specs=whole,
        scratch_shapes=[
            vmem((cols, rows), f32), vmem((width, cols), jnp.bfloat16), vmem((step, rows), f32), vmem((step, rows), f32),
            vmem((8, rows), f32), vmem((8, rows), f32), dma,
            vmem((np_, 1, 2 * rows), f32), vmem((np_, 1, rows), f32), vmem((np_, 1, rows), f32),
            vmem((nb, 1, 2 * rows), f32), vmem((nb, 1, rows), f32), vmem((nb, 1, rows), f32),
            dma((SWEEPS, np_)), dma((SWEEPS, np_)), dma((SWEEPS, nb)), dma((SWEEPS, nb)),
        ],
        compiler_params=pltpu.CompilerParams(collective_id=0, has_side_effects=True, vmem_limit_bytes=56 * 2**20),
        name="sinkhorn",
    )(teach, stud, prototypes)
    vec = jnp.concatenate(
        [sums[3:4], sums[5:6] * weight_row, weight_row / sums[0:1], jnp.zeros((5, rows), f32)], axis=0)

    half = local // 2
    step2 = min(256, half)
    block = width // nb
    stud_cols = stud.T
    other = b + 1 - 2 * lax.rem(b, 2)
    stud_t = jnp.concatenate([
        lax.dynamic_slice_in_dim(stud_cols, b * block, block, 0),
        lax.dynamic_slice_in_dim(stud_cols, other * block, block, 0)], axis=0)
    pair_rows = 2 * group_rows
    pad = -(-share // 8) * 8
    proto_grad, back = pl.pallas_call(
        functools.partial(gradient_kernel, nb, np_, half, step2, share),
        out_shape=[jax.ShapeDtypeStruct((block, local), f32), jax.ShapeDtypeStruct((share, width), f32)],
        in_specs=[whole, whole, whole, whole, pl.BlockSpec(memory_space=pl.ANY)],
        out_specs=[pl.BlockSpec(memory_space=pl.ANY), whole],
        scratch_shapes=[
            vmem((width, half), jnp.bfloat16), vmem((step2, rows), f32), vmem((step2, rows), f32),
            vmem((step2, rows), jnp.bfloat16), vmem((block, half), f32), vmem((block, half), f32),
            vmem((width, pair_rows), f32), vmem((2 * np_, pad, width), f32), vmem((2 * np_, pad, width), f32),
            dma, dma, dma, dma, dma((2 * np_,)), dma((2 * np_,)),
        ],
        compiler_params=pltpu.CompilerParams(collective_id=1, has_side_effects=True, vmem_limit_bytes=56 * 2**20),
        name="gradient",
    )(teach, stud, stud_t, vec, prototypes)
    feature_grad = own_inverse * (back - own_unit * jnp.sum(own_unit * back, axis=1, keepdims=True))
    return (feature_grad, proto_grad)


def solution(mesh):
    in_specs = (
        P("batch", None, None),
        P("batch", None, None),
        P("batch", None),
        P("batch", None),
        P(None, "proto"),
    )
    out_specs = (P(("batch", "proto"), None), P("batch", "proto"))
    run = functools.partial(on_device, mesh.shape["batch"], mesh.shape["proto"])
    return jax.shard_map(run, mesh=mesh, in_specs=in_specs, out_specs=out_specs, check_vma=False)
```

time: 643 us -> 217 us (0.34)
  waiting for transfers between devices: 385 us -> 61.9 us
  matrix products: 168 us -> 0 us
  Pallas kernels: 0 us -> 115 us
  blocking collectives: 36.1 us -> 0 us
  other arithmetic: 24.6 us -> 8.25 us
    reduce_scatter x2 -> x0, waiting for transfers between devices: 301 us -> none  [the longest x1 282 us: on_device(): lax.psum_scatter(lax.dot_general(stud_half, grad, (((0,), (0,)), ((), ())...]
    dot_general x10 -> x0, matrix products: 168 us -> none  [the longest x3 71.2 us: on_device(): row_part = jnp.dot(energy, col_scale, precision=lax.Precision.HIGHEST)]
    pallas_call x0 -> x2, Pallas kernels: none -> 115 us  [the longest x1 67.7 us: on_device(): pl.pallas_call(functools.partial(gradient_kernel, nb, np_, half, step2, s...]
    psum x3 -> x0, waiting for transfers between devices: 83.5 us -> none  [on_device(): col_scale = 1.0 / lax.psum(col_part, 'batch')]
    all_gather x0 -> x1, waiting for transfers between devices: none -> 61.9 us  [on_device(): gathered = lax.all_gather(packed, ('batch', 'proto'), axis=0, tiled=True)]
    psum x3 -> x0, blocking collectives: 36.1 us -> none  [row_total(): return lax.psum(partial_value, 'proto')]
    convert_element_type x1, other arithmetic: 16.5 us -> 0.09 us  [on_device(): teach_unit.astype(jnp.bfloat16).astype(jnp.float32)]
  transfers between devices with their start and end apart: 5 -> 1, of which waited for: 5 -> 1; matrix products, arithmetic and copies ran while one was open for 5% -> 0% of each run, Pallas kernels for 0% -> 0%
where the time goes in v1:
time: 217 us
  Pallas kernels  115 us (53%)
  waiting for transfers between devices  61.9 us (29%)
  local copies, waits for them, and re-layouts  17.5 us (8%)
  between operations  14.1 us (6%)
  other arithmetic  8.25 us (4%)
    pallas_call x1, Pallas kernels, on_device(): pl.pallas_call(functools.partial(gradient_kernel, nb, np_, half, step2, s...  67.7 us
    all_gather x1, waiting for transfers between devices, on_device(): gathered = lax.all_gather(packed, ('batch', 'proto'), axis=0, tiled=True)  61.9 us
    pallas_call x1, Pallas kernels, on_device(): pl.pallas_call(functools.partial(sinkhorn_kernel, nb, np_, cols, step), o...  47.2 us
    unnamed x4, local copies, waits for them, and re-layouts  5.21 us
  transfers between devices with their start and end apart: 1, of which 1 were waited for; matrix products, arithmetic and copies ran while one was open for 0% of the time, Pallas kernels for 0%

profile of v1, /device:TPU:7, one launch (start us, length us, event | category | flops | bytes accessed | tf_op | source)
XLA Modules:
  0.0 216.8 jit_solution(13330562303681975579)
XLA Ops:
  7.2 0.0 copy-start
  7.2 0.0 all-gather.2.cloned.1.call-start
  7.2 0.9 reduce-window.4
  8.1 0.7 fusion.14
  8.8 0.1 convert_reduce_fusion
  8.9 0.7 select_reduce_fusion.1
  9.6 0.7 copy.40
  10.3 0.7 gather_fusion
  11.1 0.0 copy-done
  11.1 0.7 gather_fusion.2
  11.8 1.7 gather_fusion.1
  13.5 0.2 fusion.7
  13.7 0.1 fusion.9
  13.8 0.1 broadcast_in_dim.60
  13.9 0.7 pad_maximum_fusion.1
  14.5 0.0 all-gather.2.cloned.1.call-update
  14.6 0.1 pad.3.clone
  14.6 61.9 %all-gather.2.cloned.1.call-done = f32[1536,640]{1,0:T(8,128)} async-done(((f32[48,640]{1,0:T(8,128)}), f32[1536,640]{1,0:T(8,128)}) %all-gather.2.cloned.1.call-update) | async-done | bytes 3932176 | tf_op jit(solution)/shard_map/all_gather | solution.py:202
  76.6 3.2 %copy.35 = bf16[1536,640]{0,1:T(8,128)(2,1)S(1)} copy(f32[1536,640]{1,0:T(8,128)} %all-gather.2.cloned.1.call-done) | data formatting | bytes 5898240 | tf_op jit(solution)/shard_map/all_gather | solution.py:202
  79.7 1.0 fusion.15
  80.7 2.3 %copy.38.teach = bf16[1536,256]{1,0:T(8,128)(2,1)} copy(bf16[1536,256]{0,1:T(8,128)(2,1)} %get-tuple-element.18) | data formatting | bytes 1572864 | tf_op jit(solution)/shard_map/slice | solution.py:203
  83.0 1.2 copy.39.stud
  84.2 0.8 pad_maximum_fusion.stud_t
  85.0 47.2 %sinkhorn.1 = f32[8,1536]{1,0:T(8,128)} custom-call(bf16[1536,256]{1,0:T(8,128)(2,1)} %copy.38.teach, bf16[1536,256]{1,0:T(8,128)(2,1)} %copy.39.stud, bf16[256,16384]{1,0:T(8,128)(2,1)} %proto.3), custom_call_target="tpu_custom_call" | custom-call | tf_op jit(solution)/shard_map/sinkhorn/pallas_call | solution.py:213
  132.1 1.4 slice_reduce_fusion
  133.5 0.9 slice_multiply_fusion
  134.5 0.7 maximum_maximum_fusion.vec
  135.2 67.7 %gradient.1 = (f32[64,16384]{1,0:T(8,128)}, f32[48,256]{1,0:T(8,128)}) custom-call(bf16[1536,256]{1,0:T(8,128)(2,1)} %copy.38.teach, bf16[1536,256]{1,0:T(8,128)(2,1)} %copy.39.stud, bf16[128,1536]{1,0:T(8,128)(2,1)} %pad_maximum_fusion.stud_t, f32[8,1536]{1,0:T(8,128)} %maximum_maximum_fusion.vec, bf16[256,16384]{1,0:T(8,128)(2,1)} %proto.3), custom_call_target="tpu_custom_call" | custom-call | tf_op jit(solution)/shard_map/gradient/pallas_call | solution.py:241
  202.9 1.0 fusion.3
  203.9 1.5 fusion.5
  205.4 4.5 %copy.42 = f32[64,16384]{1,0:T(8,128)} copy(f32[64,16384]{1,0:T(8,128)} %get-tuple-element.31) | data formatting | bytes 8388608
  (9 shorter events, 0.1 us)
Async XLA Ops:
  7.2 3.9 %copy-start = (bf16[4,256,256]{2,1,0:T(8,128)(2,1)S(1)}, bf16[4,256,256]{2,1,0:T(8,128)(2,1)}, u32[]{:S(2)}) copy-start(bf16[4,256,256]{2,1,0:T(8,128)(2,1)} %param.7) | copy-start | bytes 1572868
  7.2 69.4 %all-gather.2.cloned.1.call-start = ((), (), s32[]{:S(2)}) async-start(), calls=%async_computation | async-start | bytes 4055040 | tf_op jit(solution)/shard_map/all_gather | solution.py:202
Sparse Core Ops, SparseCore 0:
  14.7 61.8 all-gather.1

commit v2 on v0

v2 whole, which is shorter than its diff:
```python
import functools
import jax
import jax.numpy as jnp
from jax import lax
from jax.experimental import pallas as pl
from jax.experimental.pallas import tpu as pltpu
from jax.sharding import PartitionSpec as P

K = 131072
SWEEPS = 3
GROUP_ROWS = 384
LOG2E = 1.4426950408889634
MESH = pl.DeviceIdType.MESH
NT = (((1,), (1,)), ((), ()))


def unit_rows(rows):
    values = rows.astype(jnp.float32)
    inverse = lax.rsqrt(jnp.sum(values * values, axis=1, keepdims=True) + 1e-06)
    return (values * inverse, inverse)


def flip(index, bit):
    size = 2 ** bit
    return index + size - 2 * size * lax.rem(index // size, 2)


def dot_nt(left, right):
    return lax.dot_general(left, right, NT, preferred_element_type=jnp.float32)


def head_kernel(nb, np_, share, cols, step, teach_own, stud_own, weight_own, proto, out, back_out,
                teach_buf, stud_buf, weight_buf, teach, stud, stud_t, stage, energy, wbuf, ta, tb, sa, sb, ga, gb,
                acc, acc2, own, away, back, parts, mine_buf, p0, p1, p2, q0, q1, q2,
                wsem, osem, asend, arecv, bsend, brecv, psend, precv, qsend, qrecv,
                zsend, zrecv, gsend, grecv):
    b, p = lax.axis_index("batch"), lax.axis_index("proto")
    rows = teach.shape[0]
    group_rows = rows // nb
    bits = np_.bit_length() - 1
    h = lax.rem(b, 2)
    pair = b - h
    other = pair + 1 - h
    quarters = nb // 2
    mine = b // 2
    half = cols * quarters
    base = h * half
    block = out.shape[0]
    pair_rows = 2 * group_rows
    chunks = cols // step
    load = pltpu.make_async_copy(proto.at[:, pl.ds(pl.multiple_of(base, half), half)], wbuf, wsem)
    load.start()
    barrier = pltpu.get_barrier_semaphore()
    for d in range(1, np_):
        peer = lax.rem(p + d, np_)
        pl.semaphore_signal(barrier, inc=1, device_id=(b, peer), device_id_type=MESH)
        pl.semaphore_signal(barrier, inc=1, device_id=(other, peer), device_id_type=MESH)
    for d in range(1, nb):
        pl.semaphore_signal(barrier, inc=1, device_id=(lax.rem(b + d, nb), p), device_id_type=MESH)
    teach_buf[p, b] = teach_own[...]
    stud_buf[p, b] = stud_own[...]
    weight_buf[b] = weight_own[...]
    pl.semaphore_wait(barrier, 2 * (np_ - 1) + nb - 1)

    def along_batch(which, ref):
        copies = []
        for d in range(1, nb):
            copies.append(pltpu.make_async_remote_copy(
                src_ref=ref, dst_ref=ref, send_sem=zsend.at[which, d], recv_sem=zrecv.at[which, d],
                device_id=(lax.rem(b + d, nb), p), device_id_type=MESH))
        for copy in copies:
            copy.start()
        return copies

    def along_proto(which, buf, number):
        copies = []
        for part in range(2):
            outer = list(range(1, bits))
            order = (outer if part == 0 else outer[::-1]) + [0]
            held = [p]
            for bit in order[:number]:
                held = held + [flip(q, bit) for q in held]
            for k, slot in enumerate(held):
                ref = buf.at[slot, pl.ds(part * (nb // 2), nb // 2)]
                at = 2 ** number - 1 + k
                copies.append(pltpu.make_async_remote_copy(
                    src_ref=ref, dst_ref=ref, send_sem=gsend.at[which, part, at], recv_sem=grecv.at[which, part, at],
                    device_id=(b, flip(p, order[number])), device_id_type=MESH))
        for copy in copies:
            copy.start()
        return copies

    def finish(copies):
        for copy in copies:
            copy.wait()

    def round_rows(buf, target):
        for i in range(nb):
            for q in range(np_):
                stage[q * share:(q + 1) * share, :] = buf[q, i, 0:share, :]
            target[i * group_rows:(i + 1) * group_rows, :] = stage[...].astype(jnp.bfloat16)

    teach_moves = along_batch(0, teach_buf.at[p, b])
    stud_moves = along_batch(1, stud_buf.at[p, b])
    weight_moves = along_batch(2, weight_buf.at[b])
    for number in range(bits):
        finish(teach_moves)
        teach_moves = along_proto(0, teach_buf, number)
    load.wait()
    finish(stud_moves)
    finish(teach_moves)
    stud_moves = along_proto(1, stud_buf, 0)
    round_rows(teach_buf, teach)
    acc[...] = jnp.zeros_like(acc)
    acc2[...] = jnp.zeros_like(acc2)
    back[...] = jnp.zeros_like(back)

    def columns(quarter, i):
        return pl.ds(pl.multiple_of(quarter * cols + i * step, step), step)

    def pick(quarter, i):
        return wbuf[:, columns(quarter, i)].T

    def loop(low, high, one):
        if (high - low) % 2 == 0:
            def body(j, carry):
                one(low + 2 * j, 0)
                one(low + 2 * j + 1, 1)
                return carry
            lax.fori_loop(0, (high - low) // 2, body, 0)
        else:
            def body(j, carry):
                one(low + j, 0)
                return carry
            lax.fori_loop(0, high - low, body, 0)

    tbufs, sbufs, gbufs = (ta, tb), (sa, sb), (ga, gb)

    def teach_chunk(i, which):
        buf = tbufs[which]
        buf[...] = dot_nt(pick(mine, i), teach[...])
        row = acc[...]
        for g in range(0, step, 8):
            e = jnp.exp2(buf[g:g + 8, :] * (25.0 * LOG2E))
            energy[pl.ds(pl.multiple_of(i * step + g, 8), 8), :] = e
            row = row + e * (1.0 / jnp.sum(e, axis=1, keepdims=True))
        acc[...] = row

    def stud_chunk(i, which):
        buf = sbufs[which]
        buf[...] = dot_nt(pick(mine, i), stud[...])
        row = acc2[...]
        for g in range(0, step, 8):
            row = row + jnp.exp2(buf[g:g + 8, :] * (10.0 * LOG2E))
        acc2[...] = row

    for number in range(bits):
        loop(chunks * number // bits, chunks * (number + 1) // bits, teach_chunk)
        finish(stud_moves)
        if number + 1 < bits:
            stud_moves = along_proto(1, stud_buf, number + 1)
    round_rows(stud_buf, stud)
    stud_t[...] = stud[...].T
    finish(weight_moves)
    weight = jnp.concatenate([weight_buf[i] for i in range(nb)], axis=1)

    def reduce(sweep, value, pbuf, qbuf, beside):
        pbuf[p] = value
        copies = []
        for d in range(1, np_):
            copies.append(pltpu.make_async_remote_copy(
                src_ref=pbuf.at[p], dst_ref=pbuf.at[p], send_sem=psend.at[sweep, d], recv_sem=precv.at[sweep, d],
                device_id=(b, lax.rem(p + d, np_)), device_id_type=MESH))
        for copy in copies:
            copy.start()
        beside(2 * sweep)
        finish(copies)
        total = pbuf[0]
        for d in range(1, np_):
            total = total + pbuf[d]
        qbuf[b] = total
        copies = []
        for d in range(1, nb):
            copies.append(pltpu.make_async_remote_copy(
                src_ref=qbuf.at[b], dst_ref=qbuf.at[b], send_sem=qsend.at[sweep, d], recv_sem=qrecv.at[sweep, d],
                device_id=(lax.rem(b + d, nb), p), device_id_type=MESH))
        for copy in copies:
            copy.start()
        beside(2 * sweep + 1)
        finish(copies)
        total = qbuf[0]
        for d in range(1, nb):
            total = total + qbuf[d]
        return total

    gaps = 2 * (SWEEPS - 1)

    def beside(gap):
        if gap < gaps:
            loop(chunks * gap // gaps, chunks * (gap + 1) // gaps, stud_chunk)

    scale = 1.0 / reduce(0, jnp.sum(acc[...], axis=0, keepdims=True), p0, q0, beside)
    for sweep in range(1, SWEEPS):
        last = scale
        wide = jnp.broadcast_to(scale, (8, rows))

        def body(i, row):
            for g in range(0, 128, 8):
                e = energy[pl.ds(pl.multiple_of(i * 128 + g, 8), 8), :]
                row = row + e * (1.0 / jnp.sum(e * wide, axis=1, keepdims=True))
            return row

        row = jnp.sum(lax.fori_loop(0, cols // 128, body, jnp.zeros((8, rows), jnp.float32)), axis=0, keepdims=True)
        if sweep == SWEEPS - 1:
            row = jnp.concatenate([row, jnp.sum(acc2[...], axis=0, keepdims=True)], axis=1)
        total = reduce(sweep, row, (p0, p1, p2)[sweep], (q0, q1, q2)[sweep], beside)
        scale = 1.0 / total[:, :rows]
    acc[0:1, :] = last
    acc[1:2, :] = scale * weight
    acc[2:3, :] = weight / total[:, rows:]
    scale_prev, target_scale, soft_scale = acc[0:1, :], acc[1:2, :], acc[2:3, :]
    keep = stud_t[pl.ds(pl.multiple_of(mine * 2 * block, 2 * block), 2 * block), :]

    def send(quarter, i):
        at = columns(quarter, i)
        there = pl.ds(pl.multiple_of(base + quarter * cols + i * step, step), step)
        pltpu.make_async_remote_copy(
            src_ref=away.at[:, at], dst_ref=out.at[:, there], send_sem=asend, recv_sem=arecv,
            device_id=(other, p), device_id_type=MESH).start()
        pltpu.make_async_copy(own.at[:, at], out.at[:, there], osem).start()

    def gradient(quarter, i, which, known):
        s, t, grad = sbufs[which], tbufs[which], gbufs[which]
        for g in range(0, step, 16):
            if known:
                e = energy[pl.ds(pl.multiple_of(i * step + g, 16), 16), :]
            else:
                e = jnp.exp2(t[g:g + 16, :] * (25.0 * LOG2E))
            c = 1.0 / jnp.sum(e * scale_prev, axis=1, keepdims=True)
            soft = jnp.exp2(s[g:g + 16, :] * (10.0 * LOG2E)) * soft_scale
            grad[g:g + 16, :] = (soft - e * target_scale * c).astype(jnp.bfloat16)

    def products(quarter, i, which):
        at = columns(quarter, i)
        grad = gbufs[which]
        res = dot_nt(keep, grad[...])
        low, high = res[:block], res[block:]
        own[:, at] = jnp.where(h == 0, low, high)
        away[:, at] = jnp.where(h == 0, high, low)
        part = grad[:, pl.ds(pl.multiple_of(mine * pair_rows, pair_rows), pair_rows)]
        back[...] += jnp.dot(wbuf[:, at], part, preferred_element_type=jnp.float32)

    def prepare(quarter, i, which, known):
        wt = pick(quarter, i)
        sbufs[which][...] = dot_nt(wt, stud[...])
        if not known:
            tbufs[which][...] = dot_nt(wt, teach[...])

    for turn in range(quarters):
        quarter = lax.rem(mine + turn, quarters)
        known = turn == 0
        if chunks % 2 == 0:
            prepare(quarter, 0, 0, known)

            def body(j, carry):
                i = 2 * j
                prepare(quarter, i + 1, 1, known)
                gradient(quarter, i, 0, known)
                products(quarter, i, 0)
                prepare(quarter, lax.rem(i + 2, chunks), 0, known)
                gradient(quarter, i + 1, 1, known)
                products(quarter, i + 1, 1)
                send(quarter, i)
                send(quarter, i + 1)
                return carry

            lax.fori_loop(0, chunks // 2, body, 0)
        else:
            def body(i, carry):
                prepare(quarter, i, 0, known)
                gradient(quarter, i, 0, known)
                products(quarter, i, 0)
                send(quarter, i)
                return carry

            lax.fori_loop(0, chunks, body, 0)

    full = back[...].T
    for s in range(2 * np_):
        parts[s, 0:share, :] = full[s * share:(s + 1) * share, :]
    copies = []
    slot = h * np_ + p
    for d in range(1, 2 * np_):
        to = lax.rem(slot + d, 2 * np_)
        copies.append(pltpu.make_async_remote_copy(
            src_ref=parts.at[to], dst_ref=mine_buf.at[d], send_sem=bsend.at[d], recv_sem=brecv.at[d],
            device_id=(pair + to // np_, lax.rem(to, np_)), device_id_type=MESH))
    for copy in copies:
        copy.start()
    total = parts[slot]
    finish(copies)
    for d in range(1, 2 * np_):
        total = total + mine_buf[d]
    back_out[...] = total[:share]
    there = pl.ds(pl.multiple_of(base, half), half)
    pltpu.make_async_copy(own, out.at[:, there], osem).wait()
    arrive = pl.ds(pl.multiple_of(half - base, half), half)
    pltpu.make_async_remote_copy(
        src_ref=away, dst_ref=out.at[:, arrive], send_sem=asend, recv_sem=arecv,
        device_id=(other, p), device_id_type=MESH).wait()


def on_device(nb, np_, teacher, student, perm, counts, prototypes):
    img_count = teacher.shape[0]
    patches = teacher.shape[1]
    width = teacher.shape[2]
    group_rows = GROUP_ROWS
    rows = nb * group_rows
    share = group_rows // np_
    pad = -(-share // 8) * 8
    local = prototypes.shape[1]
    p = lax.axis_index("proto")
    tally = counts.reshape(-1)
    ends = jnp.cumsum(tally)
    starts = ends - tally
    line = jnp.arange(group_rows, dtype=jnp.int32)
    owner = jnp.sum((ends[None, :] <= line[:, None]).astype(jnp.int32), axis=1)
    picked = owner[:, None] == jnp.arange(img_count, dtype=jnp.int32)[None, :]
    first = jnp.sum(jnp.where(picked, starts[None, :], 0), axis=1)
    owned = jnp.sum(jnp.where(picked, tally[None, :], 0), axis=1)
    weight = ((K * 10.0) * (1.0 / owned.astype(jnp.float32))).reshape(1, group_rows)
    place = lax.dynamic_slice_in_dim(owner * patches + line - first, p * share, share, 0)
    image = lax.dynamic_slice_in_dim(owner * patches, p * share, share, 0)
    flat = image + jnp.take(perm.reshape(-1), place)
    teach_unit, unused = unit_rows(jnp.take(teacher.reshape(-1, width), flat, axis=0))
    own_unit, own_inverse = unit_rows(jnp.take(student.reshape(-1, width), flat, axis=0))
    fill = lambda x: jnp.pad(x, ((0, pad - share), (0, 0))) if pad > share else x

    cols = local // nb
    step = min(256, cols)
    half = local // 2
    block = width // nb
    pair_rows = 2 * group_rows
    vmem = pltpu.VMEM
    f32, bf16 = jnp.float32, jnp.bfloat16
    dma = pltpu.SemaphoreType.DMA
    whole = pl.BlockSpec(memory_space=vmem)
    proto_grad, back = pl.pallas_call(
        functools.partial(head_kernel, nb, np_, share, cols, step),
        out_shape=[jax.ShapeDtypeStruct((block, local), f32), jax.ShapeDtypeStruct((share, width), f32)],
        in_specs=[whole, whole, whole, pl.BlockSpec(memory_space=pl.ANY)],
        out_specs=[pl.BlockSpec(memory_space=pl.ANY), whole],
        scratch_shapes=[
            vmem((np_, nb, pad, width), f32), vmem((np_, nb, pad, width), f32), vmem((nb, 1, group_rows), f32),
            vmem((rows, width), bf16), vmem((rows, width), bf16), vmem((width, rows), bf16),
            vmem((group_rows, width), f32), vmem((cols, rows), f32), vmem((width, half), bf16),
            vmem((step, rows), f32), vmem((step, rows), f32), vmem((step, rows), f32), vmem((step, rows), f32),
            vmem((step, rows), bf16), vmem((step, rows), bf16),
            vmem((8, rows), f32), vmem((8, rows), f32),
            vmem((block, half), f32), vmem((block, half), f32),
            vmem((width, pair_rows), f32), vmem((2 * np_, pad, width), f32), vmem((2 * np_, pad, width), f32),
            vmem((np_, 1, rows), f32), vmem((np_, 1, rows), f32), vmem((np_, 1, 2 * rows), f32),
            vmem((nb, 1, rows), f32), vmem((nb, 1, rows), f32), vmem((nb, 1, 2 * rows), f32),
            dma, dma, dma, dma, dma((2 * np_,)), dma((2 * np_,)),
            dma((SWEEPS, np_)), dma((SWEEPS, np_)), dma((SWEEPS, nb)), dma((SWEEPS, nb)),
            dma((3, nb)), dma((3, nb)), dma((2, 2, np_)), dma((2, 2, np_)),
        ],
        compiler_params=pltpu.CompilerParams(collective_id=0, has_side_effects=True, vmem_limit_bytes=60 * 2**20),
        name="head",
    )(fill(teach_unit), fill(own_unit), weight, prototypes)
    feature_grad = own_inverse * (back - own_unit * jnp.sum(own_unit * back, axis=1, keepdims=True))
    return (feature_grad, proto_grad)


def solution(mesh):
    in_specs = (
        P("batch", None, None),
        P("batch", None, None),
        P("batch", None),
        P("batch", None),
        P(None, "proto"),
    )
    out_specs = (P(("batch", "proto"), None), P("batch", "proto"))
    run = functools.partial(on_device, mesh.shape["batch"], mesh.shape["proto"])
    return jax.shard_map(run, mesh=mesh, in_specs=in_specs, out_specs=out_specs, check_vma=False)
```

time: 643 us -> 145 us (0.23)
  waiting for transfers between devices: 385 us -> 0 us
  matrix products: 168 us -> 0 us
  Pallas kernels: 0 us -> 128 us
  blocking collectives: 36.1 us -> 0 us
  other arithmetic: 24.6 us -> 5.92 us
  between operations: 13.9 us -> 0.69 us
    reduce_scatter x2 -> x0, waiting for transfers between devices: 301 us -> none  [the longest x1 282 us: on_device(): lax.psum_scatter(lax.dot_general(stud_half, grad, (((0,), (0,)), ((), ())...]
    dot_general x10 -> x0, matrix products: 168 us -> none  [the longest x3 71.2 us: on_device(): row_part = jnp.dot(energy, col_scale, precision=lax.Precision.HIGHEST)]
    pallas_call x0 -> x1, Pallas kernels: none -> 128 us  [on_device(): pl.pallas_call(functools.partial(head_kernel, nb, np_, share, cols, step)...]
    psum x3 -> x0, waiting for transfers between devices: 83.5 us -> none  [on_device(): col_scale = 1.0 / lax.psum(col_part, 'batch')]
    psum x3 -> x0, blocking collectives: 36.1 us -> none  [row_total(): return lax.psum(partial_value, 'proto')]
    convert_element_type x1 -> x0, other arithmetic: 16.5 us -> none  [on_device(): (K * 10.0 * weight_row[:, None] * (soft - target)).astype(jnp.bfloat16)]
  transfers between devices with their start and end apart: 5 -> 0, of which waited for: 5 -> 0; matrix products, arithmetic and copies ran while one was open for 5% -> 0% of each run, Pallas kernels for 0% -> 0%
where the time goes in v2:
time: 145 us
  Pallas kernels  128 us (88%)
  local copies, waits for them, and re-layouts  9.97 us (7%)
  other arithmetic  5.92 us (4%)
    pallas_call x1, Pallas kernels, on_device(): pl.pallas_call(functools.partial(head_kernel, nb, np_, share, cols, step)...  128 us
    unnamed x4, local copies, waits for them, and re-layouts  6.23 us

profile of v2, /device:TPU:7, one launch (start us, length us, event | category | flops | bytes accessed | tf_op | source)
XLA Modules:
  0.0 144.7 jit_solution(12072040719642969126)
XLA Ops:
  0.6 0.0 copy-start
  0.6 1.0 copy-done
  1.7 0.7 copy.7
  2.4 0.8 reduce-window.4
  3.2 0.1 convert_reduce_fusion
  3.3 0.7 fusion.3
  3.9 0.7 select_reduce_fusion
  4.7 0.1 compare_select_fusion.1
  4.8 0.7 gather_fusion
  5.5 0.1 compare_and_fusion
  5.6 0.7 gather_fusion.1
  6.3 1.7 %gather_fusion.2 = bf16[48,256]{1,0:T(8,128)(2,1)S(1)} fusion(bf16[1024,256]{1,0:T(8,128)(2,1)} %bitcast.15, s32[1024]{0:T(1024)S(1)} %pad_clamp_fusion), kind=kCustom, calls=%fused_computation.1.clone | custom fusion | bytes 49344 | tf_op jit(solution)/shard_map/jit(_take)/gather | solution.py:335
  8.0 0.2 fusion
  8.2 0.7 convert_multiply_fusion.2
  9.0 0.6 mul.73.weight_own
  9.6 128.1 %head.1 = (f32[64,16384]{1,0:T(8,128)}, f32[48,256]{1,0:T(8,128)}) custom-call(f32[48,256]{1,0:T(8,128)} %get-tuple-element.16.teach_own, f32[48,256]{1,0:T(8,128)} %get-tuple-element.15.stud_own, f32[1,384]{1,0:T(1,128)} %mul.73.weight_own, bf16[256,16384]{1,0:T(8,128)(2,1)} %proto.1), custom_call_target="tpu_custom_call" | custom-call | tf_op jit(solution)/shard_map/head/pallas_call | solution.py:348
  137.7 1.0 multiply_reduce_fusion
  138.7 1.5 %subtract_multiply_fusion = f32[48,256]{1,0:T(8,128)} fusion(f32[48,256]{1,0:T(8,128)} %get-tuple-element.5, f32[48]{0:T(128)S(1)} %multiply_reduce_fusion, f32[48]{0:T(128)S(1)} %get-tuple-element.18, bf16[48,256]{1,0:T(8,128)(2,1)S(1)} %gather_fusion.1, pred[48]{0:T(512)(128)(4,1)S(1)} %get-tuple-element.11), kind=kLoop, calls=%fused_computation.9 | loop fusion | flops 73728 | bytes 123312 | tf_op jit(solution)/shard_map/mul | solution.py:371
  140.2 4.5 %copy.9 = f32[64,16384]{1,0:T(8,128)} copy(f32[64,16384]{1,0:T(8,128)} %get-tuple-element.22) | data formatting | bytes 8388608
  (5 shorter events, 0.0 us)
Async XLA Ops:
  0.6 1.0 copy-start

commit v3 on v2

--- a/solution.py
+++ b/solution.py
@@ -29,7 +29,7 @@
     return lax.dot_general(left, right, NT, preferred_element_type=jnp.float32)
 
 
-def head_kernel(nb, np_, share, cols, step, teach_own, stud_own, weight_own, proto, out, back_out,
+def head_kernel(nb, np_, share, cols, step, twice, teach_own, stud_own, inverse, weight_own, proto, out, feature,
                 teach_buf, stud_buf, weight_buf, teach, stud, stud_t, stage, energy, wbuf, ta, tb, sa, sb, ga, gb,
                 acc, acc2, own, away, back, parts, mine_buf, p0, p1, p2, q0, q1, q2,
                 wsem, osem, asend, arecv, bsend, brecv, psend, precv, qsend, qrecv,
@@ -48,7 +48,7 @@
     block = out.shape[0]
     pair_rows = 2 * group_rows
     chunks = cols // step
-    load = pltpu.make_async_copy(proto.at[:, pl.ds(pl.multiple_of(base, half), half)], wbuf, wsem)
+    load = pltpu.make_async_copy(proto, wbuf, wsem)
     load.start()
     barrier = pltpu.get_barrier_semaphore()
     for d in range(1, np_):
@@ -101,11 +101,12 @@
             target[i * group_rows:(i + 1) * group_rows, :] = stage[...].astype(jnp.bfloat16)
 
     teach_moves = along_batch(0, teach_buf.at[p, b])
-    stud_moves = along_batch(1, stud_buf.at[p, b])
-    weight_moves = along_batch(2, weight_buf.at[b])
     for number in range(bits):
         finish(teach_moves)
         teach_moves = along_proto(0, teach_buf, number)
+        if number == 0:
+            stud_moves = along_batch(1, stud_buf.at[p, b])
+            weight_moves = along_batch(2, weight_buf.at[b])
     load.wait()
     finish(stud_moves)
     finish(teach_moves)
@@ -115,11 +116,13 @@
     acc2[...] = jnp.zeros_like(acc2)
     back[...] = jnp.zeros_like(back)
 
-    def columns(quarter, i):
-        return pl.ds(pl.multiple_of(quarter * cols + i * step, step), step)
-
-    def pick(quarter, i):
-        return wbuf[:, columns(quarter, i)].T
+    def columns(start, i):
+        return pl.ds(pl.multiple_of(start + i * step, step), step)
+
+    def pick(start, i):
+        return wbuf[:, columns(start, i)].T
+
+    first = base + mine * cols
 
     def loop(low, high, one):
         if (high - low) % 2 == 0:
@@ -138,7 +141,7 @@
 
     def teach_chunk(i, which):
         buf = tbufs[which]
-        buf[...] = dot_nt(pick(mine, i), teach[...])
+        buf[...] = dot_nt(pick(first, i), teach[...])
         row = acc[...]
         for g in range(0, step, 8):
             e = jnp.exp2(buf[g:g + 8, :] * (25.0 * LOG2E))
@@ -148,7 +151,7 @@
 
     def stud_chunk(i, which):
         buf = sbufs[which]
-        buf[...] = dot_nt(pick(mine, i), stud[...])
+        buf[...] = dot_nt(pick(first, i), stud[...])
         row = acc2[...]
         for g in range(0, step, 8):
             row = row + jnp.exp2(buf[g:g + 8, :] * (10.0 * LOG2E))
@@ -206,8 +209,12 @@
 
         def body(i, row):
             for g in range(0, 128, 8):
-                e = energy[pl.ds(pl.multiple_of(i * 128 + g, 8), 8), :]
-                row = row + e * (1.0 / jnp.sum(e * wide, axis=1, keepdims=True))
+                at = pl.ds(pl.multiple_of(i * 128 + g, 8), 8)
+                e = energy[at, :]
+                scaled = e * (1.0 / jnp.sum(e * wide, axis=1, keepdims=True))
+                if sweep == SWEEPS - 1:
+                    energy[at, :] = scaled
+                row = row + scaled
             return row
 
         row = jnp.sum(lax.fori_loop(0, cols // 128, body, jnp.zeros((8, rows), jnp.float32)), axis=0, keepdims=True)
@@ -220,70 +227,89 @@
     acc[2:3, :] = weight / total[:, rows:]
     scale_prev, target_scale, soft_scale = acc[0:1, :], acc[1:2, :], acc[2:3, :]
     keep = stud_t[pl.ds(pl.multiple_of(mine * 2 * block, 2 * block), 2 * block), :]
-
-    def send(quarter, i):
-        at = columns(quarter, i)
-        there = pl.ds(pl.multiple_of(base + quarter * cols + i * step, step), step)
-        pltpu.make_async_remote_copy(
-            src_ref=away.at[:, at], dst_ref=out.at[:, there], send_sem=asend, recv_sem=arecv,
-            device_id=(other, p), device_id_type=MESH).start()
-        pltpu.make_async_copy(own.at[:, at], out.at[:, there], osem).start()
-
-    def gradient(quarter, i, which, known):
+    keep_own = stud_t[pl.ds(pl.multiple_of(b * block, block), block), :]
+
+    def to_other(turn, at):
+        return pltpu.make_async_remote_copy(
+            src_ref=away.at[:, at], dst_ref=out.at[:, at], send_sem=asend.at[turn], recv_sem=arecv.at[turn],
+            device_id=(other, p), device_id_type=MESH)
+
+    def to_result(turn, at):
+        return pltpu.make_async_copy(own.at[:, at], out.at[:, at], osem.at[turn])
+
+    def gradient(i, which, known):
         s, t, grad = sbufs[which], tbufs[which], gbufs[which]
         for g in range(0, step, 16):
             if known:
-                e = energy[pl.ds(pl.multiple_of(i * step + g, 16), 16), :]
+                scaled = energy[pl.ds(pl.multiple_of(i * step + g, 16), 16), :]
             else:
                 e = jnp.exp2(t[g:g + 16, :] * (25.0 * LOG2E))
-            c = 1.0 / jnp.sum(e * scale_prev, axis=1, keepdims=True)
+                scaled = e * (1.0 / jnp.sum(e * scale_prev, axis=1, keepdims=True))
             soft = jnp.exp2(s[g:g + 16, :] * (10.0 * LOG2E)) * soft_scale
-            grad[g:g + 16, :] = (soft - e * target_scale * c).astype(jnp.bfloat16)
-
-    def products(quarter, i, which):
-        at = columns(quarter, i)
+            grad[g:g + 16, :] = (soft - scaled * target_scale).astype(jnp.bfloat16)
+
+    def products(start, i, which, paired, alone):
+        at = columns(start, i)
         grad = gbufs[which]
-        res = dot_nt(keep, grad[...])
-        low, high = res[:block], res[block:]
-        own[:, at] = jnp.where(h == 0, low, high)
-        away[:, at] = jnp.where(h == 0, high, low)
-        part = grad[:, pl.ds(pl.multiple_of(mine * pair_rows, pair_rows), pair_rows)]
-        back[...] += jnp.dot(wbuf[:, at], part, preferred_element_type=jnp.float32)
-
-    def prepare(quarter, i, which, known):
-        wt = pick(quarter, i)
+        if paired:
+            res = dot_nt(keep, grad[...])
+            low, high = res[:block], res[block:]
+            own[:, at] = jnp.where(h == 0, low, high)
+            away[:, at] = jnp.where(h == 0, high, low)
+        else:
+            own[:, at] = dot_nt(keep_own, grad[...])
+        if not alone:
+            part = grad[:, pl.ds(pl.multiple_of(mine * pair_rows, pair_rows), pair_rows)]
+            back[...] += jnp.dot(wbuf[:, at], part, preferred_element_type=jnp.float32)
+
+    def prepare(start, i, which, known):
+        wt = pick(start, i)
         sbufs[which][...] = dot_nt(wt, stud[...])
         if not known:
             tbufs[which][...] = dot_nt(wt, teach[...])
 
-    for turn in range(quarters):
-        quarter = lax.rem(mine + turn, quarters)
-        known = turn == 0
-        if chunks % 2 == 0:
-            prepare(quarter, 0, 0, known)
+    def run(turn, start, low, high, known, paired, alone=False):
+        def send(i):
+            at = columns(start, i)
+            if paired:
+                to_other(turn, at).start()
+            to_result(turn, at).start()
+
+        if high == low:
+            return
+        if (high - low) % 2 == 0:
+            prepare(start, low, 0, known)
 
             def body(j, carry):
-                i = 2 * j
-                prepare(quarter, i + 1, 1, known)
-                gradient(quarter, i, 0, known)
-                products(quarter, i, 0)
-                prepare(quarter, lax.rem(i + 2, chunks), 0, known)
-                gradient(quarter, i + 1, 1, known)
-                products(quarter, i + 1, 1)
-                send(quarter, i)
-                send(quarter, i + 1)
+                i = low + 2 * j
+                prepare(start, i + 1, 1, known)
+                gradient(i, 0, known)
+                products(start, i, 0, paired, alone)
+                prepare(start, low + lax.rem(2 * j + 2, high - low), 0, known)
+                gradient(i + 1, 1, known)
+                products(start, i + 1, 1, paired, alone)
+                send(i)
+                send(i + 1)
                 return carry
 
-            lax.fori_loop(0, chunks // 2, body, 0)
+            lax.fori_loop(0, (high - low) // 2, body, 0)
         else:
-            def body(i, carry):
-                prepare(quarter, i, 0, known)
-                gradient(quarter, i, 0, known)
-                products(quarter, i, 0)
-                send(quarter, i)
+            def body(j, carry):
+                prepare(start, low + j, 0, known)
+                gradient(low + j, 0, known)
+                products(start, low + j, 0, paired, alone)
+                send(low + j)
                 return carry
 
-            lax.fori_loop(0, chunks, body, 0)
+            lax.fori_loop(0, high - low, body, 0)
+
+    sent = chunks - twice
+    starts = [lax.rem(mine + turn, quarters) * cols for turn in range(quarters)]
+    run(0, base + starts[0], 0, chunks, True, True)
+    for turn in range(1, quarters):
+        run(turn, base + starts[turn], 0, sent, False, True)
+    for turn in range(1, quarters):
+        run(turn, base + starts[turn], sent, chunks, False, False)
 
     full = back[...].T
     for s in range(2 * np_):
@@ -297,17 +323,24 @@
             device_id=(pair + to // np_, lax.rem(to, np_)), device_id_type=MESH))
     for copy in copies:
         copy.start()
+    there = half - base
+    for turn in range(1, quarters):
+        run(quarters + turn, there + starts[turn], sent, chunks, False, False, True)
     total = parts[slot]
     finish(copies)
     for d in range(1, 2 * np_):
         total = total + mine_buf[d]
-    back_out[...] = total[:share]
-    there = pl.ds(pl.multiple_of(base, half), half)
-    pltpu.make_async_copy(own, out.at[:, there], osem).wait()
-    arrive = pl.ds(pl.multiple_of(half - base, half), half)
-    pltpu.make_async_remote_copy(
-        src_ref=away, dst_ref=out.at[:, arrive], send_sem=asend, recv_sem=arecv,
-        device_id=(other, p), device_id_type=MESH).wait()
+    unit = stud_own[...]
+    full_back = inverse[...] * (total - unit * jnp.sum(unit * total, axis=1, keepdims=True))
+    feature[...] = full_back[:share]
+    for turn in range(quarters):
+        span = cols if turn == 0 else sent * step
+        to_result(turn, pl.ds(pl.multiple_of(base + starts[turn], cols), cols)).wait()
+        if span > 0:
+            to_other(turn, pl.ds(pl.multiple_of(base + starts[turn], cols), span)).wait_send()
+            to_other(turn, pl.ds(pl.multiple_of(there + starts[turn], cols), span)).wait_recv()
+        if turn > 0 and twice > 0:
+            to_result(quarters + turn, pl.ds(pl.multiple_of(there + starts[turn] + sent * step, step), twice * step)).wait()
 
 
 def on_device(nb, np_, teacher, student, perm, counts, prototypes):
@@ -321,7 +354,8 @@
     local = prototypes.shape[1]
     p = lax.axis_index("proto")
     tally = counts.reshape(-1)
-    ends = jnp.cumsum(tally)
+    order = jnp.arange(img_count, dtype=jnp.int32)
+    ends = jnp.sum(jnp.where(order[None, :] <= order[:, None], tally[None, :], 0), axis=1)
     starts = ends - tally
     line = jnp.arange(group_rows, dtype=jnp.int32)
     owner = jnp.sum((ends[None, :] <= line[:, None]).astype(jnp.int32), axis=1)
@@ -338,37 +372,37 @@
 
     cols = local // nb
     step = min(256, cols)
-    half = local // 2
+    quarters = nb // 2
+    twice = cols // step // 2
     block = width // nb
     pair_rows = 2 * group_rows
     vmem = pltpu.VMEM
     f32, bf16 = jnp.float32, jnp.bfloat16
     dma = pltpu.SemaphoreType.DMA
     whole = pl.BlockSpec(memory_space=vmem)
-    proto_grad, back = pl.pallas_call(
-        functools.partial(head_kernel, nb, np_, share, cols, step),
+    proto_grad, feature_grad = pl.pallas_call(
+        functools.partial(head_kernel, nb, np_, share, cols, step, twice),
         out_shape=[jax.ShapeDtypeStruct((block, local), f32), jax.ShapeDtypeStruct((share, width), f32)],
-        in_specs=[whole, whole, whole, pl.BlockSpec(memory_space=pl.ANY)],
+        in_specs=[whole, whole, whole, whole, pl.BlockSpec(memory_space=pl.ANY)],
         out_specs=[pl.BlockSpec(memory_space=pl.ANY), whole],
         scratch_shapes=[
             vmem((np_, nb, pad, width), f32), vmem((np_, nb, pad, width), f32), vmem((nb, 1, group_rows), f32),
             vmem((rows, width), bf16), vmem((rows, width), bf16), vmem((width, rows), bf16),
-            vmem((group_rows, width), f32), vmem((cols, rows), f32), vmem((width, half), bf16),
+            vmem((group_rows, width), f32), vmem((cols, rows), f32), vmem((width, local), bf16),
             vmem((step, rows), f32), vmem((step, rows), f32), vmem((step, rows), f32), vmem((step, rows), f32),
             vmem((step, rows), bf16), vmem((step, rows), bf16),
             vmem((8, rows), f32), vmem((8, rows), f32),
-            vmem((block, half), f32), vmem((block, half), f32),
+            vmem((block, local), f32), vmem((block, local), f32),
             vmem((width, pair_rows), f32), vmem((2 * np_, pad, width), f32), vmem((2 * np_, pad, width), f32),
             vmem((np_, 1, rows), f32), vmem((np_, 1, rows), f32), vmem((np_, 1, 2 * rows), f32),
             vmem((nb, 1, rows), f32), vmem((nb, 1, rows), f32), vmem((nb, 1, 2 * rows), f32),
-            dma, dma, dma, dma, dma((2 * np_,)), dma((2 * np_,)),
+            dma, dma((2 * quarters,)), dma((quarters,)), dma((quarters,)), dma((2 * np_,)), dma((2 * np_,)),
             dma((SWEEPS, np_)), dma((SWEEPS, np_)), dma((SWEEPS, nb)), dma((SWEEPS, nb)),
             dma((3, nb)), dma((3, nb)), dma((2, 2, np_)), dma((2, 2, np_)),
         ],
         compiler_params=pltpu.CompilerParams(collective_id=0, has_side_effects=True, vmem_limit_bytes=60 * 2**20),
         name="head",
-    )(fill(teach_unit), fill(own_unit), weight, prototypes)
-    feature_grad = own_inverse * (back - own_unit * jnp.sum(own_unit * back, axis=1, keepdims=True))
+    )(fill(teach_unit), fill(own_unit), fill(own_inverse), weight, prototypes)
     return (feature_grad, proto_grad)
 
 

time: 145 us -> 177 us (1.22)
  Pallas kernels: 128 us -> 160 us
  other arithmetic: 5.92 us -> 3.36 us
  local copies, waits for them, and re-layouts: 9.97 us -> 12.1 us
    pallas_call x1, Pallas kernels: 128 us -> 160 us  [on_device(): pl.pallas_call(functools.partial(head_kernel, nb, np_, share, cols, step,...]
    unnamed x4 -> x5, local copies, waits for them, and re-layouts: 6.23 us -> 7.65 us
where the time goes in v3:
time: 177 us; the launch traced here: 176 us
  Pallas kernels  160 us (90%)
  local copies, waits for them, and re-layouts  12.1 us (7%)
  other arithmetic  3.36 us (2%)
    pallas_call x1, Pallas kernels, on_device(): pl.pallas_call(functools.partial(head_kernel, nb, np_, share, cols, step,...  160 us
    unnamed x5, local copies, waits for them, and re-layouts  7.65 us

profile of v3, /device:TPU:7, one launch (start us, length us, event | category | flops | bytes accessed | tf_op | source)
XLA Modules:
  0.0 176.2 jit_solution(13700660362231990845)
XLA Ops:
  0.6 0.0 copy-start
  0.6 1.0 copy-done
  1.7 0.8 select_reduce_fusion.2
  2.4 0.7 fusion.3
  3.1 0.1 convert_reduce_fusion
  3.2 0.7 select_reduce_fusion
  3.9 0.6 mul.56.weight_own
  4.5 0.1 compare_select_fusion.1
  4.6 0.7 copy.10
  5.3 0.7 gather_fusion
  6.0 0.1 compare_and_fusion
  6.1 0.7 gather_fusion.2
  6.8 1.7 gather_fusion.1
  8.5 0.2 fusion.1
  8.7 0.7 copy.9.inverse
  9.4 0.7 convert_multiply_fusion
  10.2 160.1 %head.1 = (f32[64,16384]{1,0:T(8,128)}, f32[48,256]{1,0:T(8,128)}) custom-call(f32[48,256]{1,0:T(8,128)} %get-tuple-element.18.teach_own, f32[48,256]{1,0:T(8,128)} %get-tuple-element.17.stud_own, f32[48,1]{1,0:T(8,128)} %copy.9.inverse, f32[1,384]{1,0:T(1,128)} %mul.56.weight_own, bf16[256,16384]{1,0:T(8,128)(2,1)} %proto.1), custom_call_target="tpu_custom_call" | custom-call | tf_op jit(solution)/shard_map/head/pallas_call | solution.py:383
  170.3 1.4 copy.13
  171.7 4.5 %copy.14 = f32[64,16384]{1,0:T(8,128)} copy(f32[64,16384]{1,0:T(8,128)} %get-tuple-element.23) | data formatting | bytes 8388608
  (5 shorter events, 0.0 us)
Async XLA Ops:
  0.6 1.0 copy-start

commit v4 on v3

--- a/solution.py
+++ b/solution.py
@@ -212,8 +212,6 @@
                 at = pl.ds(pl.multiple_of(i * 128 + g, 8), 8)
                 e = energy[at, :]
                 scaled = e * (1.0 / jnp.sum(e * wide, axis=1, keepdims=True))
-                if sweep == SWEEPS - 1:
-                    energy[at, :] = scaled
                 row = row + scaled
             return row
 
@@ -239,14 +237,21 @@
 
     def gradient(i, which, known):
         s, t, grad = sbufs[which], tbufs[which], gbufs[which]
+
+        def held(g):
+            return energy[pl.ds(pl.multiple_of(i * step + g, 16), 16), :] if known else t[g:g + 16, :]
+
+        col_scale = []
         for g in range(0, step, 16):
             if known:
-                scaled = energy[pl.ds(pl.multiple_of(i * step + g, 16), 16), :]
+                e = held(g)
             else:
                 e = jnp.exp2(t[g:g + 16, :] * (25.0 * LOG2E))
-                scaled = e * (1.0 / jnp.sum(e * scale_prev, axis=1, keepdims=True))
+                t[g:g + 16, :] = e
+            col_scale.append(1.0 / jnp.sum(e * scale_prev, axis=1, keepdims=True))
+        for g in range(0, step, 16):
             soft = jnp.exp2(s[g:g + 16, :] * (10.0 * LOG2E)) * soft_scale
-            grad[g:g + 16, :] = (soft - scaled * target_scale).astype(jnp.bfloat16)
+            grad[g:g + 16, :] = (soft - held(g) * target_scale * col_scale[g // 16]).astype(jnp.bfloat16)
 
     def products(start, i, which, paired, alone):
         at = columns(start, i)
@@ -373,7 +378,7 @@
     cols = local // nb
     step = min(256, cols)
     quarters = nb // 2
-    twice = cols // step // 2
+    twice = cols // step // 4
     block = width // nb
     pair_rows = 2 * group_rows
     vmem = pltpu.VMEM

time: 177 us -> 137 us (0.77)
  Pallas kernels: 160 us -> 120 us
    pallas_call x1, Pallas kernels: 160 us -> 120 us  [on_device(): pl.pallas_call(functools.partial(head_kernel, nb, np_, share, cols, step,...]
where the time goes in v4:
time: 137 us; the launch traced here: 136 us
  Pallas kernels  120 us (88%)
  local copies, waits for them, and re-layouts  12.1 us (9%)
  other arithmetic  3.36 us (2%)
    pallas_call x1, Pallas kernels, on_device(): pl.pallas_call(functools.partial(head_kernel, nb, np_, share, cols, step,...  120 us
    unnamed x5, local copies, waits for them, and re-layouts  7.65 us

profile of v4, /device:TPU:7, one launch (start us, length us, event | category | flops | bytes accessed | tf_op | source)
XLA Modules:
  0.0 136.5 jit_solution(10361368189056598480)
XLA Ops:
  0.6 0.0 copy-start
  0.6 1.0 copy-done
  1.7 0.8 select_reduce_fusion.2
  2.4 0.7 fusion.3
  3.1 0.1 convert_reduce_fusion
  3.2 0.7 select_reduce_fusion
  3.9 0.6 mul.56.weight_own
  4.5 0.1 compare_select_fusion.1
  4.6 0.7 copy.10
  5.3 0.7 gather_fusion
  6.0 0.1 compare_and_fusion
  6.1 0.7 gather_fusion.2
  6.8 1.7 %gather_fusion.1 = bf16[48,256]{1,0:T(8,128)(2,1)S(1)} fusion(bf16[1024,256]{1,0:T(8,128)(2,1)} %bitcast.15, s32[1024]{0:T(1024)S(1)} %pad_clamp_fusion), kind=kCustom, calls=%fused_computation.clone | custom fusion | bytes 49344 | tf_op jit(solution)/shard_map/jit(_take)/gather | solution.py:374
  8.5 0.2 fusion.1
  8.7 0.7 copy.9.inverse
  9.4 0.7 convert_multiply_fusion
  10.2 120.4 %head.1 = (f32[64,16384]{1,0:T(8,128)}, f32[48,256]{1,0:T(8,128)}) custom-call(f32[48,256]{1,0:T(8,128)} %get-tuple-element.18.teach_own, f32[48,256]{1,0:T(8,128)} %get-tuple-element.17.stud_own, f32[48,1]{1,0:T(8,128)} %copy.9.inverse, f32[1,384]{1,0:T(1,128)} %mul.56.weight_own, bf16[256,16384]{1,0:T(8,128)(2,1)} %proto.1), custom_call_target="tpu_custom_call" | custom-call | tf_op jit(solution)/shard_map/head/pallas_call | solution.py:388
  130.5 1.4 %copy.13 = f32[48,256]{1,0:T(8,128)} copy(f32[48,256]{1,0:T(8,128)} %get-tuple-element.22) | data formatting | bytes 98304
  132.0 4.5 %copy.14 = f32[64,16384]{1,0:T(8,128)} copy(f32[64,16384]{1,0:T(8,128)} %get-tuple-element.23) | data formatting | bytes 8388608
  (5 shorter events, 0.0 us)
Async XLA Ops:
  0.6 1.0 copy-start
